TPU v7x, 32 devices: a whole 2x2x4 slice. The times are simulated.
32 devices in a mesh: sec: 2 (over x), blk: 8 (over z, y), head: 2 (over core).
Axes of the slice: x: 2, y: 2, z: 4, core: 2. Of those that a mesh axis runs over, the one named last changes fastest.
Arguments:
- tokens: bfloat16 [8192, 768], P(('sec', 'blk')), parts along dimension 0, may hold values from -6 to 6
- counts: int32 [16], P(('sec', 'blk')), parts along dimension 0, may hold values from 128 to 512, as said below
- face_owner: int32 [6, 8192], P(None, ('sec', 'blk')), parts along dimension 1, may hold values from 0 to 7, as said below
- face_row: int32 [6, 8192], P(None, ('sec', 'blk')), parts along dimension 1, may hold values from 0 to 511, as said below
- face_count: int32 [8192], P(('sec', 'blk')), parts along dimension 0, may hold values from 1 to 6
- mix_weight: bfloat16 [768, 768], P(None, 'head'), may hold values from -0.21875 to 0.21875
- norm_gain: bfloat16 [768], replicated, may hold values from 0.25 to 1.75
- query_weight: bfloat16 [768, 768], P(None, 'head'), may hold values from -1 to 1
- key_weight: bfloat16 [768, 768], P(None, 'head'), may hold values from -1 to 1
- value_weight: bfloat16 [768, 768], P(None, 'head'), may hold values from -0.21875 to 0.21875
- out_weight: bfloat16 [768, 768], P('head'), may hold values from -0.21875 to 0.21875
Outputs:
- layer_out: bfloat16 [8192, 768], P(('sec', 'blk'), 'head'), parts along dimension 0
There are 2 independent parts, one for each index of `sec`. A program takes and returns all parts, laid end to end along the dimension named above; an argument that names none is the same for every part. Nothing has to cross between parts.
Inputs may be any that keep to these rules, and one draw needn't show every extreme that they name: `counts`: each section has one block with exactly 512 live tokens and one with exactly 128. `face_owner`: A token's face neighbours lie in its own block or in the blocks one index below or above it, the last block's above being block 0. `face_row`: A face neighbour is a live slot of its owner's block.
All inputs are finite; a program needn't handle non-finite values.
Results may differ from a plain program's by a relative error of at most 0.012.
The roundings to bfloat16 on the way count: a program that leaves them out, or rounds other values in their place, can miss the bound.
Values may be sent and summed in bfloat16 or wider, within the bound.
A program may use at most 64 MiB of HBM per device.

v0:
```python
import jax
import jax.numpy as jnp
from jax import lax
from jax.sharding import PartitionSpec as P

HS = 64


def extended_2(array, sides, width):
    for axis, dim in sides:
        size, length = (lax.axis_size(axis), array.shape[dim])
        up = [(i, (i + 1) % size) for i in range(size)]
        down = [(j, i) for i, j in up]
        last = lax.slice_in_dim(array, length - width, length, axis=dim)
        first = lax.slice_in_dim(array, 0, width, axis=dim)
        before = lax.ppermute(last, axis, up)
        after = lax.ppermute(first, axis, down)
        array = jnp.concatenate([before, array, after], axis=dim)
    return array


def rms_norm(values, gain):
    var = jnp.mean(values * values, axis=-1, keepdims=True)
    return values * lax.rsqrt(var + 1e-05) * gain


def local(
    tokens,
    counts,
    face_owner,
    face_row,
    face_count,
    mix_weight,
    norm_gain,
    query_weight,
    key_weight,
    value_weight,
    out_weight,
):
    rows = tokens.shape[0]
    faces = face_owner.shape[0]
    cycle_size = lax.axis_size("blk")
    place = lax.axis_index("blk")
    half = mix_weight.shape[1]
    head_place = lax.axis_index("head")
    extended = extended_2(tokens, (("blk", 0),), rows)
    offset = (face_owner - place + 1 + cycle_size) % cycle_size
    local_rows = offset * rows + face_row
    picked = extended[local_rows]
    live = lax.broadcasted_iota(jnp.int32, (faces, rows), 0) < face_count[None, :]
    picked = jnp.where(live[:, :, None], picked, jnp.zeros((), jnp.bfloat16))
    summed = jnp.sum(picked, axis=0, dtype=jnp.float32)
    summed = (summed / face_count[:, None].astype(jnp.float32)).astype(jnp.bfloat16)
    own_tokens = lax.dynamic_slice_in_dim(tokens, head_place * half, half, 1)
    own_mixed = own_tokens.astype(jnp.float32) + jnp.dot(
        summed, mix_weight, preferred_element_type=jnp.float32
    )
    stream = lax.all_gather(own_mixed.astype(jnp.bfloat16), "head", axis=1, tiled=True)
    normed = rms_norm(stream.astype(jnp.float32), norm_gain.astype(jnp.float32)).astype(
        jnp.bfloat16
    )
    heads = query_weight.shape[1] // HS
    scale = 1.0 / HS**0.5
    query = jnp.dot(normed, query_weight, preferred_element_type=jnp.float32).astype(jnp.bfloat16)
    query_heads = query.reshape(rows, heads, HS)

    def attend_block(carry, block):
        top, total, acc = carry
        keys, values, live_count = block
        key_heads = keys.reshape(rows, heads, HS)
        value_heads = values.reshape(rows, heads, HS)
        key_live = lax.broadcasted_iota(jnp.int32, (rows,), 0) < live_count
        scores = (
            jnp.einsum("qhd,khd->hqk", query_heads, key_heads, preferred_element_type=jnp.float32)
            * scale
        )
        scores = jnp.where(key_live[None, None, :], scores, -1e30)
        new_top = jnp.maximum(top, jnp.max(scores, axis=-1))
        fade = jnp.exp(top - new_top)
        probs = jnp.where(key_live[None, None, :], jnp.exp(scores - new_top[:, :, None]), 0.0)
        total = total * fade + jnp.sum(probs, axis=-1)
        update = jnp.einsum(
            "hqk,khd->hqd",
            probs.astype(jnp.bfloat16),
            value_heads,
            preferred_element_type=jnp.float32,
        )
        acc = acc * fade[:, :, None] + update
        return ((new_top, total, acc), None)

    start_carry = (
        jnp.full((heads, rows), -1e30, jnp.float32),
        jnp.zeros((heads, rows), jnp.float32),
        jnp.zeros((heads, rows, HS), jnp.float32),
    )
    key = jnp.dot(normed, key_weight, preferred_element_type=jnp.float32).astype(jnp.bfloat16)
    value = jnp.dot(normed, value_weight, preferred_element_type=jnp.float32).astype(jnp.bfloat16)
    carry = start_carry
    keys = lax.all_gather(key, "blk", axis=0, tiled=True)
    values = lax.all_gather(value, "blk", axis=0, tiled=True)
    live_piece = lax.all_gather(counts, "blk", axis=0, tiled=True)
    shards = live_piece.shape[0]
    blocks = (keys.reshape(shards, rows, -1), values.reshape(shards, rows, -1), live_piece)
    carry, unused = lax.scan(attend_block, carry, blocks)
    top, total, acc = carry
    context = acc / total[:, :, None]
    context = context.transpose(1, 0, 2).reshape(rows, heads * HS).astype(jnp.bfloat16)
    own_stream = lax.dynamic_slice_in_dim(stream, head_place * half, half, 1)
    partial_out = jnp.dot(context, out_weight, preferred_element_type=jnp.float32)
    head_total = lax.psum_scatter(
        partial_out.astype(jnp.bfloat16), "head", scatter_dimension=1, tiled=True
    ).astype(jnp.float32)
    return (own_stream.astype(jnp.float32) + head_total).astype(jnp.bfloat16)


def solution(mesh):
    in_specs = (
        P(("sec", "blk"), None),
        P(("sec", "blk")),
        P(None, ("sec", "blk")),
        P(None, ("sec", "blk")),
        P(("sec", "blk")),
        P(None, "head"),
        P(),
        P(None, "head"),
        P(None, "head"),
        P(None, "head"),
        P("head", None),
    )
    out_specs = P(("sec", "blk"), "head")
    return jax.shard_map(local, mesh=mesh, in_specs=in_specs, out_specs=out_specs, check_vma=False)
```

profile of v0, /device:TPU:0, one launch (start us, length us, event | category | flops | bytes accessed | tf_op | source)
XLA Modules:
  0.0 282.3 jit_solution(9265060979988700921)
XLA Ops:
  6.5 3.0 %collective-permute-start = (bf16[512,768]{1,0:T(8,128)(2,1)}, bf16[512,768]{1,0:T(8,128)(2,1)S(1)}, u32[]{:S(2)}, u32[]{:S(2)}) collective-permute-start(bf16[512,768]{1,0:T(8,128)(2,1)} %param.13), channel_id=1, source_target_pairs={{0,2},{2,4},{4,6},{6,8},{8,10},{10,12},{12,14},{14,0},{1,3},{3,5},... | collective-permute-start | bytes 2359304 | tf_op jit(solution)/shard_map/ppermute | solution.py:16
  9.5 3.0 %collective-permute-start.1 = (bf16[512,768]{1,0:T(8,128)(2,1)}, bf16[512,768]{1,0:T(8,128)(2,1)}, u32[]{:S(2)}, u32[]{:S(2)}) collective-permute-start(bf16[512,768]{1,0:T(8,128)(2,1)} %param.13), channel_id=1, source_target_pairs={{2,0},{4,2},{6,4},{8,6},{10,8},{12,10},{14,12},{0,14},{3,1},{5,3},... | collective-permute-start | bytes 2359304 | tf_op jit(solution)/shard_map/ppermute | solution.py:17
  15.4 28.1 %collective-permute-done = bf16[512,768]{1,0:T(8,128)(2,1)S(1)} collective-permute-done((bf16[512,768]{1,0:T(8,128)(2,1)}, bf16[512,768]{1,0:T(8,128)(2,1)S(1)}, u32[]{:S(2)}, u32[]{:S(2)}) %collective-permute-start) | collective-permute-done | bytes 786464 | tf_op jit(solution)/shard_map/ppermute | solution.py:16
  45.7 1.8 pad_maximum_fusion
  47.4 13.6 %gather_fusion = bf16[3072,768]{1,0:T(8,128)(2,1)} fusion(bf16[1536,768]{1,0:T(8,128)(2,1)S(1)} %pad_maximum_fusion, s32[3072]{0:T(1024)S(1)} %broadcast_clamp_fusion), kind=kCustom, calls=%fused_computation | custom fusion | bytes 9449472 | tf_op jit(solution)/shard_map/gather | solution.py:49
  61.1 3.1 %convert_reduce_fusion = f32[512,768]{1,0:T(8,128)S(1)} fusion(bf16[6,512,768]{2,1,0:T(8,128)(2,1)} %bitcast.55, pred[6,512]{1,0:T(8,128)(4,1)S(1)} %iota_compare_fusion.1), kind=kLoop, calls=%fused_computation.23 | loop fusion | flops 6684672 | bytes 6294528 | tf_op jit(solution)/shard_map/reduce_sum | solution.py:52
  64.9 2.5 all_gather.12
  72.6 11.3 %all-reduce = s32[8]{0:T(128)S(1)} all-reduce(s32[8]{0:T(128)S(1)} %dynamic-update-slice), channel_id=1, replica_groups=mesh['sec'=2,'blk'=8,'head'=2] {'blk'}, use_global_device_ids=true, to_apply=%add | all-reduce | flops 8 | bytes 64
  85.6 44.9 %all-gather.5.cloned.1.call-done = bf16[4096,384]{1,0:T(8,128)(2,1)} async-done(((bf16[512,384]{1,0:T(8,128)(2,1)}), bf16[4096,384]{1,0:T(8,128)(2,1)}) %all-gather.5.cloned.1.call-update) | async-done | bytes 3145744 | tf_op jit(solution)/shard_map/all_gather | solution.py:100
  130.5 61.3 %all-gather.3.cloned.1.call-done = bf16[4096,384]{1,0:T(8,128)(2,1)} async-done(((bf16[512,384]{1,0:T(8,128)(2,1)}), bf16[4096,384]{1,0:T(8,128)(2,1)}) %all-gather.3.cloned.1.call-update) | async-done | bytes 3145744 | tf_op jit(solution)/shard_map/all_gather | solution.py:99
  191.8 71.9 %while.15 = (s32[]{:T(128)}, f32[6,512]{1,0:T(8,128)S(1)}, f32[6,512]{1,0:T(8,128)S(1)}, f32[6,512,64]{1,2,0:T(8,128)}, s32[8]{0:T(128)S(1)}, /*index=5*/bf16[8,...) while((s32[]{:T(128)}, f32[6,512]{1,0:T(8,128)S(1)}, ...), condition=%wide.region_5.6_spmd.clone, body=%wide.region_2.5_spmd.clone.sunk | while | flops 423706112 | bytes 31262916 | solution.py:104
  196.2 1.9 fusion.45
  205.2 1.9 fusion.45
  207.2 1.7 fusion.47
  214.2 1.9 fusion.45
  216.2 1.7 fusion.47
  223.2 1.9 fusion.45
  225.1 1.7 fusion.47
  232.2 1.9 fusion.45
  241.2 1.9 fusion.45
  250.1 1.9 fusion.45
  259.1 1.9 fusion.45
  261.1 1.7 fusion.47
  266.7 7.0 %reduce-scatter.4.cloned.1.call-done = bf16[384,512]{1,0:T(8,128)(2,1)} async-done(((bf16[768,512]{1,0:T(8,128)(2,1)}), bf16[384,512]{1,0:T(8,128)(2,1)}) %reduce-scatter.4.cloned.1.call-update) | async-done | bytes 393232
  (152 shorter events, 65.9 us)
Async XLA Ops:
  6.5 258.4 %copy-start = (bf16[384,768]{1,0:T(8,128)(2,1)S(1)}, bf16[384,768]{1,0:T(8,128)(2,1)}, u32[]{:S(2)}) copy-start(bf16[384,768]{1,0:T(8,128)(2,1)} %param.23) | copy-start | bytes 1769476
  6.5 124.0 %all-gather.5.cloned.1.call-start = ((), (), s32[]{:S(2)}) async-start(), calls=%async_computation.2 | async-start | bytes 3538944 | tf_op jit(solution)/shard_map/all_gather | solution.py:100
  6.5 36.9 %collective-permute-start = (bf16[512,768]{1,0:T(8,128)(2,1)}, bf16[512,768]{1,0:T(8,128)(2,1)S(1)}, u32[]{:S(2)}, u32[]{:S(2)}) collective-permute-start(bf16[512,768]{1,0:T(8,128)(2,1)} %param.13), channel_id=1, source_target_pairs={{0,2},{2,4},{4,6},{6,8},{8,10},{10,12},{12,14},{14,0},{1,3},{3,5},... | collective-permute-start | bytes 2359304 | tf_op jit(solution)/shard_map/ppermute | solution.py:16
  9.5 36.2 %collective-permute-start.1 = (bf16[512,768]{1,0:T(8,128)(2,1)}, bf16[512,768]{1,0:T(8,128)(2,1)}, u32[]{:S(2)}, u32[]{:S(2)}) collective-permute-start(bf16[512,768]{1,0:T(8,128)(2,1)} %param.13), channel_id=1, source_target_pairs={{2,0},{4,2},{6,4},{8,6},{10,8},{12,10},{14,12},{0,14},{3,1},{5,3},... | collective-permute-start | bytes 2359304 | tf_op jit(solution)/shard_map/ppermute | solution.py:17
  61.1 3.2 %copy-start.1 = (bf16[512,768]{1,0:T(8,128)(2,1)S(1)}, bf16[512,768]{1,0:T(8,128)(2,1)}, u32[]{:S(2)}) copy-start(bf16[512,768]{1,0:T(8,128)(2,1)} %param.13) | copy-start | bytes 2359300
  61.1 3.2 %copy-start.5 = (bf16[768,384]{1,0:T(8,128)(2,1)S(1)}, bf16[768,384]{1,0:T(8,128)(2,1)}, u32[]{:S(2)}) copy-start(bf16[768,384]{1,0:T(8,128)(2,1)} %param.18) | copy-start | bytes 1769476
  64.2 3.4 %copy-start.6 = (bf16[768,384]{1,0:T(8,128)(2,1)S(1)}, bf16[768,384]{1,0:T(8,128)(2,1)}, u32[]{:S(2)}) copy-start(bf16[768,384]{1,0:T(8,128)(2,1)} %param.22) | copy-start | bytes 1769476
  64.9 4.2 %copy-start.7 = (bf16[768,384]{1,0:T(8,128)(2,1)S(1)}, bf16[768,384]{1,0:T(8,128)(2,1)}, u32[]{:S(2)}) copy-start(bf16[768,384]{1,0:T(8,128)(2,1)} %param.21) | copy-start | bytes 1769476
  67.6 3.6 %copy-start.8 = (u32[32]{0:T(128)S(1)}, u32[32]{0:T(128)}, u32[]{:S(2)}) copy-start(u32[32]{0:T(128)} %constant.69) | copy-start | bytes 388
  69.1 122.7 %all-gather.3.cloned.1.call-start = ((), (), s32[]{:S(2)}) async-start(), calls=%async_computation.1 | async-start | bytes 3538944 | tf_op jit(solution)/shard_map/all_gather | solution.py:99
  70.5 203.2 %reduce-scatter.4.cloned.1.call-start = ((), (), s32[]{:S(2)}) async-start(), calls=%async_computation.3 | async-start | bytes 1179648
  196.2 1.9 copy-start.3
  199.9 0.9 copy-start.4
  205.2 1.9 copy-start.3
  208.9 0.9 copy-start.4
  214.2 1.9 copy-start.3
  217.9 0.9 copy-start.4
  223.2 1.9 copy-start.3
  226.9 0.9 copy-start.4
  232.2 1.9 copy-start.3
  235.8 0.9 copy-start.4
  241.2 1.9 copy-start.3
  250.1 1.9 copy-start.3
  259.1 1.9 copy-start.3
  (4 other events, 3.6 us)
Sparse Core Ops, SparseCore 0:
  69.2 61.2 all-gather.4
  132.7 59.0 all-gather.2
  266.9 6.8 reduce-scatter.3
where the time goes:
time: 283 us; the launch traced here: 282 us
  waiting for transfers between devices  143 us (51%)
  local copies, waits for them, and re-layouts  42.6 us (15%)
  matrix products  31.8 us (11%)
  other arithmetic  30.6 us (11%)
  between operations  13.9 us (5%)
  blocking collectives  13.8 us (5%)
  starting transfers between devices  6.09 us (2%)
    all_gather x1, waiting for transfers between devices, local(): keys = lax.all_gather(key, 'blk', axis=0, tiled=True)  61.3 us
    all_gather x1, waiting for transfers between devices, local(): values = lax.all_gather(value, 'blk', axis=0, tiled=True)  44.9 us
    ppermute x1, waiting for transfers between devices, extended_2(): before = lax.ppermute(last, axis, up)  28.1 us
    dynamic_slice x32, local copies, waits for them, and re-layouts, local(): carry, unused = lax.scan(attend_block, carry, blocks)  17.3 us
    reduce_sum x8, other arithmetic, attend_block(): total = total * fade + jnp.sum(probs, axis=-1)  15.3 us
    dot_general x8, matrix products, attend_block(): jnp.einsum('hqk,khd->hqd', probs.astype(jnp.bfloat16), value_heads, prefe...  13.7 us
    gather x1, local copies, waits for them, and re-layouts, local(): picked = extended[local_rows]  13.6 us
    dot_general x8, matrix products, attend_block(): jnp.einsum('qhd,khd->hqk', query_heads, key_heads, preferred_element_type...  12.5 us
  transfers between devices with their start and end apart: 5, of which 5 were waited for; matrix products, arithmetic and copies ran while one was open for 3% of the time, Pallas kernels for 0%

commit v1 on v0

v1 whole, which is shorter than its diff:
```python
import functools
import math

import jax
import jax.numpy as jnp
from jax import lax
from jax.experimental import pallas as pl
from jax.experimental.pallas import tpu as pltpu
from jax.sharding import PartitionSpec as P

MESH = pl.DeviceIdType.MESH
HS = 64
NT = (((1,), (1,)), ((), ()))
F32 = jnp.float32
BF16 = jnp.bfloat16


def kernel(
    n, lanes_y,
    tokens, counts, face_owner, face_row, face_count, gain, mix_w, query_w, key_w, value_w, out_w,
    out,
    ext, own_rows, onehot, pack, summed, all_normed, stream_half, count_all,
    mix_full, wq, wk, wv, wvt, wo, qm, vt, acc, top, sent_out, got_out, own_out,
    local_sem, halo_send, halo_recv, mix_sem, sum_sem, count_send, count_recv,
    z_send, z_recv, y_send, y_recv, sib_send, sib_recv, stream_sem, out_sem,
):
    rows, width = tokens.shape
    half_w = width // 2
    half_r = rows // 2
    heads = half_w // HS
    faces = face_owner.shape[0]
    b = lax.axis_index("blk")
    c = lax.axis_index("head")
    other = 1 - c
    nz = n // lanes_y
    zi, yi = b // lanes_y, b % lanes_y
    my_rows = pl.ds(pl.multiple_of(c * half_r, half_r), half_r)
    sib_rows = pl.ds(pl.multiple_of(other * half_r, half_r), half_r)
    my_cols = pl.ds(pl.multiple_of(c * half_w, 128), half_w)
    sib_cols = pl.ds(pl.multiple_of(other * half_w, 128), half_w)

    def remote(src, dst, send, recv, **where):
        return pltpu.make_async_remote_copy(
            src_ref=src, dst_ref=dst, send_sem=send, recv_sem=recv,
            device_id=where, device_id_type=MESH,
        )

    loads = [
        pltpu.make_async_copy(tokens.at[:, my_cols], ext.at[1], local_sem.at[0]),
        pltpu.make_async_copy(tokens.at[my_rows, :], own_rows, local_sem.at[1]),
        pltpu.make_async_copy(mix_w, mix_full.at[:, my_cols], local_sem.at[2]),
        pltpu.make_async_copy(query_w, wq, local_sem.at[3]),
        pltpu.make_async_copy(key_w, wk, local_sem.at[4]),
        pltpu.make_async_copy(value_w, wv, local_sem.at[5]),
        pltpu.make_async_copy(out_w, wo, local_sem.at[6]),
    ]

    barrier = pltpu.get_barrier_semaphore()
    for j in range(1, n):
        pl.semaphore_signal(barrier, inc=1, device_id={"blk": (b + j) % n}, device_id_type=MESH)
    pl.semaphore_signal(barrier, inc=1, device_id={"head": other}, device_id_type=MESH)
    pl.semaphore_wait(barrier, n)

    up, down = (b + 1) % n, (b + n - 1) % n
    halo_up = remote(tokens.at[:, my_cols], ext.at[0], halo_send.at[0], halo_recv.at[0], blk=up)
    halo_down = remote(tokens.at[:, my_cols], ext.at[2], halo_send.at[1], halo_recv.at[1], blk=down)
    halo_up.start()
    halo_down.start()
    mix_copy = remote(mix_w, mix_full.at[:, my_cols], mix_sem.at[0], mix_sem.at[1], head=other)
    mix_copy.start()
    for load in loads:
        load.start()

    count_all[b] = jnp.full((8, 128), counts[0], jnp.int32)

    def count_copy(j):
        return remote(
            count_all.at[b], count_all.at[b], count_send.at[j], count_recv.at[j], blk=(b + j) % n
        )

    for j in range(1, n):
        count_copy(j).start()

    off = face_owner[...] - b + 1
    off = jnp.where(off < 0, off + n, off)
    off = jnp.where(off >= n, off - n, off)
    index = off * rows + face_row[...]
    face = lax.broadcasted_iota(jnp.int32, (faces, rows), 0)
    index = jnp.where(face < face_count[...], index, -1)
    pack[...] = jnp.zeros_like(pack)
    pack[0:faces, :] = index.astype(F32)
    pack[faces : faces + 1, :] = face_count[...].astype(F32)
    pack_t = pack[...].T
    face_total = pack_t[:, faces : faces + 1]
    for s in range(3):
        place = (lax.broadcasted_iota(jnp.int32, (rows, rows), 1) + s * rows).astype(F32)
        total = jnp.zeros((rows, rows), F32)
        for f in range(faces):
            total = total + jnp.where(pack_t[:, f : f + 1] == place, 1.0, 0.0)
        onehot[:, s * rows : (s + 1) * rows] = total.astype(BF16)

    for load in loads:
        load.wait()
    wvt[...] = wv[...].astype(F32).T.astype(BF16)
    acc[...] = jnp.zeros_like(acc)
    top[...] = jnp.full_like(top, -1e30)

    part = jnp.dot(onehot[:, rows : 2 * rows], ext[1], preferred_element_type=F32)
    halo_up.wait()
    part += jnp.dot(onehot[:, 0:rows], ext[0], preferred_element_type=F32)
    halo_down.wait()
    part += jnp.dot(onehot[:, 2 * rows :], ext[2], preferred_element_type=F32)
    summed[:, my_cols] = (part / face_total).astype(BF16)
    sum_copy = remote(
        summed.at[sib_rows, my_cols], summed.at[sib_rows, my_cols], sum_sem.at[0], sum_sem.at[1],
        head=other,
    )
    sum_copy.start()
    mix_copy.wait()
    sum_copy.wait()
    stream = own_rows[...].astype(F32) + jnp.dot(
        summed[my_rows, :], mix_full[...], preferred_element_type=F32
    )
    own_rows[...] = stream.astype(BF16)
    stream = own_rows[...].astype(F32)
    var = jnp.mean(stream * stream, axis=-1, keepdims=True)
    all_normed[b, my_rows, :] = (stream * lax.rsqrt(var + 1e-05) * gain[...].astype(F32)).astype(
        BF16
    )

    def half(block):
        return all_normed.at[block, my_rows]

    def z_copy(block, direction):
        step = 2 * direction - 1
        return remote(
            half(block), half(block), z_send.at[direction, block // lanes_y],
            z_recv.at[block // lanes_y], blk=b + step * lanes_y,
        )

    def y_copy(block):
        return remote(
            half(block), half(block), y_send.at[block // lanes_y], y_recv.at[block // lanes_y],
            blk=zi * lanes_y + (lanes_y - 1 - yi),
        )

    def sib_copy(block):
        return remote(
            half(block), half(block), sib_send.at[block], sib_recv.at[block], head=other
        )

    def sib_arrival(block):
        return remote(
            all_normed.at[block, sib_rows], all_normed.at[block, sib_rows],
            sib_send.at[block], sib_recv.at[block], head=other,
        )

    near = jnp.minimum(zi, nz - 1 - zi)
    far_sign = jnp.where(zi < nz - 1 - zi, 1, -1)

    def line(k):
        close = zi + (1 - 2 * (k % 2)) * ((k + 1) // 2)
        return jnp.where(k <= 2 * near, close, zi + far_sign * (k - near))

    def on_line(k):
        z = line(k)
        block = z * lanes_y + yi

        @pl.when(k > 0)
        def _():
            z_copy(block, 1).wait_recv()

        @pl.when((z <= zi) & (zi < nz - 1))
        def _():
            z_copy(block, 1).start()

        @pl.when((z >= zi) & (zi > 0))
        def _():
            z_copy(block, 0).start()

        if lanes_y > 1:
            y_copy(block).start()
        sib_copy(block).start()
        return block

    def across(k):
        block = line(k) * lanes_y + (lanes_y - 1 - yi)
        y_copy(block).wait_recv()
        sib_copy(block).start()
        return block

    def attend(block):
        live = count_all[block]
        normed = all_normed[block]
        live_row = lax.broadcasted_iota(jnp.int32, (rows, half_w), 0) < live[0:1, 0:1]
        keys = jnp.dot(normed, wk[...], preferred_element_type=F32)
        keys = jnp.where(live_row, keys, keys[0:1, :]).astype(BF16)
        live_col = lax.broadcasted_iota(jnp.int32, (half_w, rows), 1) < live[0:1, 0:1]
        values = lax.dot_general(wvt[...], normed, NT, preferred_element_type=F32)
        values = jnp.where(live_col, values, 0.0).astype(BF16)
        ones = jnp.where(live_col[0:16, :], 1.0, 0.0).astype(BF16)
        for h in range(heads):
            pair = (h // 2) * 2 * HS
            vt[h, 0:HS, :] = values[h * HS : (h + 1) * HS, :]
            vt[h, HS:, :] = ones
            scores = lax.dot_general(
                keys[:, pair : pair + 2 * HS], qm[h], NT, preferred_element_type=F32
            )
            old = top[h : h + 1, :]
            new = jnp.maximum(old, jnp.max(scores, axis=0, keepdims=True))
            probs = jnp.exp2(scores - new).astype(BF16)
            top[h : h + 1, :] = new
            acc[h] = acc[h] * jnp.exp2(old - new) + jnp.dot(
                vt[h], probs, preferred_element_type=F32
            )

    on_line(0)
    stream_half[my_rows, :] = own_rows[:, my_cols]
    stream_copy = remote(
        own_rows.at[:, sib_cols], stream_half.at[my_rows], stream_sem.at[0], stream_sem.at[1],
        head=other,
    )
    stream_copy.start()
    for j in range(1, n):
        count_copy(j).wait()
    sib_arrival(b).wait_recv()
    query = jnp.dot(all_normed[b], wq[...], preferred_element_type=F32) * (
        math.log2(math.e) / HS**0.5
    )
    lane = lax.broadcasted_iota(jnp.int32, (rows, 2 * HS), 1) // HS
    for h in range(heads):
        pair = (h // 2) * 2 * HS
        qm[h] = jnp.where(lane == h % 2, query[:, pair : pair + 2 * HS], 0.0).astype(BF16)

    attend(b)

    if lanes_y > 1:

        def step(i, carry):
            is_line = (i % 2 == 1) & (i < n - 1)
            k = jnp.where(is_line, (i + 1) // 2, i // 2 - 1 + (i // (n - 1)) * (nz - 1 - (i // 2 - 1)))

            @pl.when(is_line)
            def _():
                on_line(k)

            @pl.when(jnp.logical_not(is_line))
            def _():
                across(k)

            block = line(k) * lanes_y + jnp.where(is_line, yi, lanes_y - 1 - yi)
            sib_arrival(block).wait_recv()
            attend(block)
            return carry

    else:

        def step(i, carry):
            block = on_line(i)
            sib_arrival(block).wait_recv()
            attend(block)
            return carry

    lax.fori_loop(1, n, step, 0)

    context = []
    for h in range(heads):
        context.append(acc[h, 0:HS, :] / acc[h, HS : HS + 1, :])
    context = jnp.concatenate(context, axis=0).T.astype(BF16)
    sent_out[...] = jnp.dot(context, wo[:, sib_cols], preferred_element_type=F32).astype(BF16)
    out_copy = remote(sent_out, got_out, out_sem.at[0], out_sem.at[1], head=other)
    out_copy.start()
    mine = jnp.dot(context, wo[:, my_cols], preferred_element_type=F32)
    stream_copy.wait()
    mine = mine + stream_half[...].astype(F32)
    out_copy.wait()
    out[...] = (mine + got_out[...].astype(F32)).astype(BF16)

    def drain(k, carry):
        z = line(k)
        block = z * lanes_y + yi

        @pl.when((z <= zi) & (zi < nz - 1))
        def _():
            z_copy(block, 1).wait_send()

        @pl.when((z >= zi) & (zi > 0))
        def _():
            z_copy(block, 0).wait_send()

        if lanes_y > 1:
            y_copy(block).wait_send()
            sib_copy(z * lanes_y + (lanes_y - 1 - yi)).wait_send()
        sib_copy(block).wait_send()
        return carry

    lax.fori_loop(0, nz, drain, 0)


def local(n, lanes_y, tokens, counts, face_owner, face_row, face_count, mix_w, gain, query_w, key_w, value_w, out_w):
    rows, width = tokens.shape
    half_w = width // 2
    heads = half_w // HS
    nz = n // lanes_y
    any_, vmem = pl.BlockSpec(memory_space=pl.ANY), pl.BlockSpec(memory_space=pltpu.VMEM)
    smem = pl.BlockSpec(memory_space=pltpu.SMEM)
    sem = pltpu.SemaphoreType.DMA
    return pl.pallas_call(
        functools.partial(kernel, n, lanes_y),
        out_shape=jax.ShapeDtypeStruct((rows, half_w), BF16),
        in_specs=[any_, smem, vmem, vmem, vmem, vmem, any_, any_, any_, any_, any_],
        out_specs=vmem,
        scratch_shapes=[
            pltpu.VMEM((3, rows, half_w), BF16),
            pltpu.VMEM((rows // 2, width), BF16),
            pltpu.VMEM((rows, 3 * rows), BF16),
            pltpu.VMEM((128, rows), F32),
            pltpu.VMEM((rows, width), BF16),
            pltpu.VMEM((n, rows, width), BF16),
            pltpu.VMEM((rows, half_w), BF16),
            pltpu.VMEM((n, 8, 128), jnp.int32),
            pltpu.VMEM((width, width), BF16),
            pltpu.VMEM((width, half_w), BF16),
            pltpu.VMEM((width, half_w), BF16),
            pltpu.VMEM((width, half_w), BF16),
            pltpu.VMEM((half_w, width), BF16),
            pltpu.VMEM((half_w, width), BF16),
            pltpu.VMEM((heads, rows, 2 * HS), BF16),
            pltpu.VMEM((heads, HS + 16, rows), BF16),
            pltpu.VMEM((heads, HS + 16, rows), F32),
            pltpu.VMEM((8, rows), F32),
            pltpu.VMEM((rows, half_w), BF16),
            pltpu.VMEM((rows, half_w), BF16),
            pltpu.VMEM((rows, half_w), F32),
            sem((7,)), sem((2,)), sem((2,)), sem((2,)), sem((2,)), sem((n,)), sem((n,)),
            sem((2, nz)), sem((nz,)), sem((nz,)), sem((nz,)), sem((n,)), sem((n,)), sem((2,)), sem((2,)),
        ],
        compiler_params=pltpu.CompilerParams(
            collective_id=0, has_side_effects=True, vmem_limit_bytes=50 * 2**20
        ),
    )(
        tokens, counts, face_owner, face_row, face_count[None, :], gain[None, :],
        mix_w, query_w, key_w, value_w, out_w,
    )


def solution(mesh):
    n = mesh.shape["blk"]
    lanes_y = 2 if n == 8 else 1
    rows = P(("sec", "blk"), None)
    in_specs = (
        rows, P(("sec", "blk")), P(None, ("sec", "blk")), P(None, ("sec", "blk")),
        P(("sec", "blk")), P(None, "head"), P(), P(None, "head"), P(None, "head"),
        P(None, "head"), P("head", None),
    )
    return jax.shard_map(
        functools.partial(local, n, lanes_y), mesh=mesh, in_specs=in_specs,
        out_specs=P(("sec", "blk"), "head"), check_vma=False,
    )
```

time: 283 us -> 96.3 us (0.34)
  waiting for transfers between devices: 143 us -> 0 us
  Pallas kernels: 0 us -> 87 us
  local copies, waits for them, and re-layouts: 42.6 us -> 8.19 us
  matrix products: 31.8 us -> 0 us
  other arithmetic: 30.6 us -> 0 us
  blocking collectives: 13.8 us -> 0 us
  between operations: 13.9 us -> 0.7 us
  starting transfers between devices: 6.09 us -> 0 us
    all_gather x2 -> x0, waiting for transfers between devices: 106 us -> none  [the longest x1 61.3 us: local(): keys = lax.all_gather(key, 'blk', axis=0, tiled=True)]
    pallas_call x0 -> x1, Pallas kernels: none -> 87 us  [local(): pl.pallas_call(functools.partial(kernel, n, lanes_y), out_shape=jax.Shape...]
    dot_general x21 -> x0, matrix products: 31.8 us -> none  [the longest x8 13.7 us: attend_block(): jnp.einsum('hqk,khd->hqd', probs.astype(jnp.bfloat16), value_heads, prefe...]
    ppermute x2 -> x0, waiting for transfers between devices: 29.4 us -> none  [the longest x1 28.1 us: extended_2(): before = lax.ppermute(last, axis, up)]
    reduce_sum x10 -> x0, other arithmetic: 18.6 us -> none  [the longest x8 15.3 us: attend_block(): total = total * fade + jnp.sum(probs, axis=-1)]
    dynamic_slice x32 -> x0, local copies, waits for them, and re-layouts: 17.3 us -> none  [local(): carry, unused = lax.scan(attend_block, carry, blocks)]
    gather x1 -> x0, local copies, waits for them, and re-layouts: 13.6 us -> none  [local(): picked = extended[local_rows]]
    unnamed x1 -> x0, blocking collectives: 11.3 us -> none
  transfers between devices with their start and end apart: 5 -> 0, of which waited for: 5 -> 0; matrix products, arithmetic and copies ran while one was open for 3% -> 0% of each run, Pallas kernels for 0% -> 0%
where the time goes in v1:
time: 96.3 us; the launch traced here: 95.8 us
  Pallas kernels  87 us (90%)
  local copies, waits for them, and re-layouts  8.19 us (9%)
    pallas_call x1, Pallas kernels, local(): pl.pallas_call(functools.partial(kernel, n, lanes_y), out_shape=jax.Shape...  87 us
    unnamed x19, local copies, waits for them, and re-layouts  8.18 us

profile of v1, /device:TPU:0, one launch (start us, length us, event | category | flops | bytes accessed | tf_op | source)
XLA Modules:
  0.0 95.8 jit_solution(5124131094193063933)
XLA Ops:
  0.0 0.0 copy-start.8
  0.7 0.0 copy-done.8
  0.7 0.0 copy-start.7
  0.7 0.7 copy-done.7
  1.4 0.0 copy-start
  1.4 1.1 %copy-done = bf16[768,384]{1,0:T(8,128)(2,1)S(1)} copy-done((bf16[768,384]{1,0:T(8,128)(2,1)S(1)}, bf16[768,384]{1,0:T(8,128)(2,1)}, u32[]{:S(2)}) %copy-start) | copy-done | bytes 589848
  2.4 0.0 copy-start.1
  2.4 1.1 %copy-done.1 = bf16[768,384]{1,0:T(8,128)(2,1)S(1)} copy-done((bf16[768,384]{1,0:T(8,128)(2,1)S(1)}, bf16[768,384]{1,0:T(8,128)(2,1)}, u32[]{:S(2)}) %copy-start.1) | copy-done | bytes 589848
  3.5 0.0 copy-start.2
  3.5 1.1 %copy-done.2 = bf16[768,384]{1,0:T(8,128)(2,1)S(1)} copy-done((bf16[768,384]{1,0:T(8,128)(2,1)S(1)}, bf16[768,384]{1,0:T(8,128)(2,1)}, u32[]{:S(2)}) %copy-start.2) | copy-done | bytes 589848
  4.6 0.0 copy-start.3
  4.6 1.1 %copy-done.3 = bf16[768,384]{1,0:T(8,128)(2,1)S(1)} copy-done((bf16[768,384]{1,0:T(8,128)(2,1)S(1)}, bf16[768,384]{1,0:T(8,128)(2,1)}, u32[]{:S(2)}) %copy-start.3) | copy-done | bytes 589848
  5.6 0.0 copy-start.4
  5.6 1.1 %copy-done.4 = bf16[384,768]{1,0:T(8,128)(2,1)S(1)} copy-done((bf16[384,768]{1,0:T(8,128)(2,1)S(1)}, bf16[384,768]{1,0:T(8,128)(2,1)}, u32[]{:S(2)}) %copy-start.4) | copy-done | bytes 589848
  6.7 0.0 copy-start.5
  6.7 0.7 copy-done.5
  7.4 0.0 copy-start.6
  7.4 0.7 copy-done.6
  8.1 87.0 %shard_map.109 = bf16[512,384]{1,0:T(8,128)(2,1)S(1)} custom-call(bf16[512,768]{1,0:T(8,128)(2,1)} %tokens.1, s32[1]{0:T(128)S(6)} %copy.13.counts, s32[6,512]{1,0:T(8,128)S(1)} %copy-done.5, s32[6,512]{1,0:T(8,128)S(1)} %copy-done.6, s32[1,512]{1,0:T(1,128)S(1)} %bitcast.1, bf16[1,768]{1,0:T(2,128)(2,1)S(1)} %broadcast_in_dim.7.gain, ...), custom_call_target="tpu_custom_call" | custom-call | tf_op jit(solution)/shard_map/pallas_call | solution.py:308
  95.1 0.7 copy.14
  (1 shorter events, 0.0 us)
Async XLA Ops:
  0.0 0.7 copy-start.8
  0.7 0.7 copy-start.7
  1.4 1.1 %copy-start = (bf16[768,384]{1,0:T(8,128)(2,1)S(1)}, bf16[768,384]{1,0:T(8,128)(2,1)}, u32[]{:S(2)}) copy-start(bf16[768,384]{1,0:T(8,128)(2,1)} %mix_w.1) | copy-start | bytes 1769476
  2.4 1.1 %copy-start.1 = (bf16[768,384]{1,0:T(8,128)(2,1)S(1)}, bf16[768,384]{1,0:T(8,128)(2,1)}, u32[]{:S(2)}) copy-start(bf16[768,384]{1,0:T(8,128)(2,1)} %query_w.1) | copy-start | bytes 1769476
  3.5 1.1 %copy-start.2 = (bf16[768,384]{1,0:T(8,128)(2,1)S(1)}, bf16[768,384]{1,0:T(8,128)(2,1)}, u32[]{:S(2)}) copy-start(bf16[768,384]{1,0:T(8,128)(2,1)} %key_w.1) | copy-start | bytes 1769476
  4.6 1.1 %copy-start.3 = (bf16[768,384]{1,0:T(8,128)(2,1)S(1)}, bf16[768,384]{1,0:T(8,128)(2,1)}, u32[]{:S(2)}) copy-start(bf16[768,384]{1,0:T(8,128)(2,1)} %value_w.1) | copy-start | bytes 1769476
  5.6 1.1 %copy-start.4 = (bf16[384,768]{1,0:T(8,128)(2,1)S(1)}, bf16[384,768]{1,0:T(8,128)(2,1)}, u32[]{:S(2)}) copy-start(bf16[384,768]{1,0:T(8,128)(2,1)} %out_w.1) | copy-start | bytes 1769476
  6.7 0.7 copy-start.5
  7.4 0.7 copy-start.6

commit v2 on v1

--- a/solution.py
+++ b/solution.py
@@ -20,13 +20,14 @@
     tokens, counts, face_owner, face_row, face_count, gain, mix_w, query_w, key_w, value_w, out_w,
     out,
     ext, own_rows, onehot, pack, summed, all_normed, stream_half, count_all,
-    mix_full, wq, wk, wv, wvt, wo, qm, vt, acc, top, sent_out, got_out, own_out,
+    mix_full, wq, wk, wv, wvt, wo, qm, vt, acc, top, sent_out, got_out,
     local_sem, halo_send, halo_recv, mix_sem, sum_sem, count_send, count_recv,
     z_send, z_recv, y_send, y_recv, sib_send, sib_recv, stream_sem, out_sem,
 ):
     rows, width = tokens.shape
     half_w = width // 2
     half_r = rows // 2
+    piece = half_r // 2
     heads = half_w // HS
     faces = face_owner.shape[0]
     b = lax.axis_index("blk")
@@ -128,31 +129,33 @@
         BF16
     )
 
-    def half(block):
-        return all_normed.at[block, my_rows]
-
-    def z_copy(block, direction):
+    def chunk(block, ch):
+        return all_normed.at[block, pl.ds(pl.multiple_of(c * half_r + ch * piece, piece), piece)]
+
+    def z_copy(block, ch, direction):
         step = 2 * direction - 1
         return remote(
-            half(block), half(block), z_send.at[direction, block // lanes_y],
-            z_recv.at[block // lanes_y], blk=b + step * lanes_y,
-        )
-
-    def y_copy(block):
-        return remote(
-            half(block), half(block), y_send.at[block // lanes_y], y_recv.at[block // lanes_y],
-            blk=zi * lanes_y + (lanes_y - 1 - yi),
-        )
-
-    def sib_copy(block):
-        return remote(
-            half(block), half(block), sib_send.at[block], sib_recv.at[block], head=other
-        )
-
-    def sib_arrival(block):
-        return remote(
-            all_normed.at[block, sib_rows], all_normed.at[block, sib_rows],
-            sib_send.at[block], sib_recv.at[block], head=other,
+            chunk(block, ch), chunk(block, ch), z_send.at[direction, block // lanes_y, ch],
+            z_recv.at[block // lanes_y, ch], blk=b + step * lanes_y,
+        )
+
+    def y_copy(block, ch):
+        return remote(
+            chunk(block, ch), chunk(block, ch), y_send.at[block // lanes_y, ch],
+            y_recv.at[block // lanes_y, ch], blk=zi * lanes_y + (lanes_y - 1 - yi),
+        )
+
+    def sib_copy(block, ch):
+        return remote(
+            chunk(block, ch), chunk(block, ch), sib_send.at[block, ch], sib_recv.at[block, ch],
+            head=other,
+        )
+
+    def sib_arrival(block, ch):
+        place = pl.ds(pl.multiple_of(other * half_r + ch * piece, piece), piece)
+        return remote(
+            all_normed.at[block, place], all_normed.at[block, place],
+            sib_send.at[block, ch], sib_recv.at[block, ch], head=other,
         )
 
     near = jnp.minimum(zi, nz - 1 - zi)
@@ -162,32 +165,28 @@
         close = zi + (1 - 2 * (k % 2)) * ((k + 1) // 2)
         return jnp.where(k <= 2 * near, close, zi + far_sign * (k - near))
 
-    def on_line(k):
+    def on_line(k, ch, first=False):
         z = line(k)
         block = z * lanes_y + yi
-
-        @pl.when(k > 0)
-        def _():
-            z_copy(block, 1).wait_recv()
+        if not first:
+            z_copy(block, ch, 1).wait_recv()
 
         @pl.when((z <= zi) & (zi < nz - 1))
         def _():
-            z_copy(block, 1).start()
+            z_copy(block, ch, 1).start()
 
         @pl.when((z >= zi) & (zi > 0))
         def _():
-            z_copy(block, 0).start()
+            z_copy(block, ch, 0).start()
 
         if lanes_y > 1:
-            y_copy(block).start()
-        sib_copy(block).start()
-        return block
-
-    def across(k):
+            y_copy(block, ch).start()
+        sib_copy(block, ch).start()
+
+    def across(k, ch):
         block = line(k) * lanes_y + (lanes_y - 1 - yi)
-        y_copy(block).wait_recv()
-        sib_copy(block).start()
-        return block
+        y_copy(block, ch).wait_recv()
+        sib_copy(block, ch).start()
 
     def attend(block):
         live = count_all[block]
@@ -200,12 +199,20 @@
         values = jnp.where(live_col, values, 0.0).astype(BF16)
         ones = jnp.where(live_col[0:16, :], 1.0, 0.0).astype(BF16)
         for h in range(heads):
-            pair = (h // 2) * 2 * HS
             vt[h, 0:HS, :] = values[h * HS : (h + 1) * HS, :]
             vt[h, HS:, :] = ones
-            scores = lax.dot_general(
+
+        def score(h):
+            pair = (h // 2) * 2 * HS
+            return lax.dot_general(
                 keys[:, pair : pair + 2 * HS], qm[h], NT, preferred_element_type=F32
             )
+
+        ahead = score(0)
+        for h in range(heads):
+            scores = ahead
+            if h + 1 < heads:
+                ahead = score(h + 1)
             old = top[h : h + 1, :]
             new = jnp.maximum(old, jnp.max(scores, axis=0, keepdims=True))
             probs = jnp.exp2(scores - new).astype(BF16)
@@ -214,7 +221,8 @@
                 vt[h], probs, preferred_element_type=F32
             )
 
-    on_line(0)
+    on_line(0, 0, True)
+    on_line(0, 1, True)
     stream_half[my_rows, :] = own_rows[:, my_cols]
     stream_copy = remote(
         own_rows.at[:, sib_cols], stream_half.at[my_rows], stream_sem.at[0], stream_sem.at[1],
@@ -223,7 +231,8 @@
     stream_copy.start()
     for j in range(1, n):
         count_copy(j).wait()
-    sib_arrival(b).wait_recv()
+    for ch in range(2):
+        sib_arrival(b, ch).wait_recv()
     query = jnp.dot(all_normed[b], wq[...], preferred_element_type=F32) * (
         math.log2(math.e) / HS**0.5
     )
@@ -232,36 +241,39 @@
         pair = (h // 2) * 2 * HS
         qm[h] = jnp.where(lane == h % 2, query[:, pair : pair + 2 * HS], 0.0).astype(BF16)
 
-    attend(b)
-
-    if lanes_y > 1:
-
-        def step(i, carry):
-            is_line = (i % 2 == 1) & (i < n - 1)
-            k = jnp.where(is_line, (i + 1) // 2, i // 2 - 1 + (i // (n - 1)) * (nz - 1 - (i // 2 - 1)))
-
-            @pl.when(is_line)
+    last = 2 * nz + 1 if lanes_y > 1 else 2 * nz - 1
+
+    def step(s, carry):
+        k, ch = s // 2, s % 2
+
+        @pl.when((k > 0) & (k < nz))
+        def _():
+            on_line(k, ch)
+
+        if lanes_y > 1:
+
+            @pl.when(k > 0)
             def _():
-                on_line(k)
-
-            @pl.when(jnp.logical_not(is_line))
+                across(k - 1, ch)
+
+            on_own = (ch == 1) & (k < nz)
+            place = jnp.where(on_own, k, jnp.maximum(k - 2 + ch, 0))
+            block = line(place) * lanes_y + jnp.where(on_own, yi, lanes_y - 1 - yi)
+        else:
+            block = line(k)
+
+        @pl.when((s != 2) if lanes_y > 1 else (ch == 1))
+        def _():
+            @pl.when(s > 1)
             def _():
-                across(k)
-
-            block = line(k) * lanes_y + jnp.where(is_line, yi, lanes_y - 1 - yi)
-            sib_arrival(block).wait_recv()
+                for piece_index in range(2):
+                    sib_arrival(block, piece_index).wait_recv()
+
             attend(block)
-            return carry
-
-    else:
-
-        def step(i, carry):
-            block = on_line(i)
-            sib_arrival(block).wait_recv()
-            attend(block)
-            return carry
-
-    lax.fori_loop(1, n, step, 0)
+
+        return carry
+
+    lax.fori_loop(1, last + 1, step, 0)
 
     context = []
     for h in range(heads):
@@ -276,25 +288,26 @@
     out_copy.wait()
     out[...] = (mine + got_out[...].astype(F32)).astype(BF16)
 
-    def drain(k, carry):
+    def drain(s, carry):
+        k, ch = s // 2, s % 2
         z = line(k)
         block = z * lanes_y + yi
 
         @pl.when((z <= zi) & (zi < nz - 1))
         def _():
-            z_copy(block, 1).wait_send()
+            z_copy(block, ch, 1).wait_send()
 
         @pl.when((z >= zi) & (zi > 0))
         def _():
-            z_copy(block, 0).wait_send()
+            z_copy(block, ch, 0).wait_send()
 
         if lanes_y > 1:
-            y_copy(block).wait_send()
-            sib_copy(z * lanes_y + (lanes_y - 1 - yi)).wait_send()
-        sib_copy(block).wait_send()
+            y_copy(block, ch).wait_send()
+            sib_copy(z * lanes_y + (lanes_y - 1 - yi), ch).wait_send()
+        sib_copy(block, ch).wait_send()
         return carry
 
-    lax.fori_loop(0, nz, drain, 0)
+    lax.fori_loop(0, 2 * nz, drain, 0)
 
 
 def local(n, lanes_y, tokens, counts, face_owner, face_row, face_count, mix_w, gain, query_w, key_w, value_w, out_w):
@@ -331,12 +344,12 @@
             pltpu.VMEM((8, rows), F32),
             pltpu.VMEM((rows, half_w), BF16),
             pltpu.VMEM((rows, half_w), BF16),
-            pltpu.VMEM((rows, half_w), F32),
             sem((7,)), sem((2,)), sem((2,)), sem((2,)), sem((2,)), sem((n,)), sem((n,)),
-            sem((2, nz)), sem((nz,)), sem((nz,)), sem((nz,)), sem((n,)), sem((n,)), sem((2,)), sem((2,)),
+            sem((2, nz, 2)), sem((nz, 2)), sem((nz, 2)), sem((nz, 2)), sem((n, 2)), sem((n, 2)),
+            sem((2,)), sem((2,)),
         ],
         compiler_params=pltpu.CompilerParams(
-            collective_id=0, has_side_effects=True, vmem_limit_bytes=50 * 2**20
+            collective_id=0, has_side_effects=True, vmem_limit_bytes=60 * 2**20
         ),
     )(
         tokens, counts, face_owner, face_row, face_count[None, :], gain[None, :],

time: 96.3 us -> 79.8 us (0.83)
  Pallas kernels: 87 us -> 76.5 us
  local copies, waits for them, and re-layouts: 8.19 us -> 2.38 us
    pallas_call x1, Pallas kernels: 87 us -> 76.5 us  [local(): pl.pallas_call(functools.partial(kernel, n, lanes_y), out_shape=jax.Shape...]
    unnamed x19 -> x3, local copies, waits for them, and re-layouts: 8.18 us -> 1.8 us
where the time goes in v2:
time: 79.8 us; the launch traced here: 79.5 us
  Pallas kernels  76.5 us (96%)
  local copies, waits for them, and re-layouts  2.38 us (3%)
    pallas_call x1, Pallas kernels, local(): pl.pallas_call(functools.partial(kernel, n, lanes_y), out_shape=jax.Shape...  76.5 us
    unnamed x3, local copies, waits for them, and re-layouts  1.8 us

profile of v2, /device:TPU:0, one launch (start us, length us, event | category | flops | bytes accessed | tf_op | source)
XLA Modules:
  0.0 79.5 jit_solution(3666833234259267796)
XLA Ops:
  0.0 0.0 copy-start
  0.7 0.0 copy-done
  0.7 0.6 broadcast_in_dim.7.gain
  1.3 76.5 %shard_map.109 = bf16[512,384]{1,0:T(8,128)(2,1)} custom-call(bf16[512,768]{1,0:T(8,128)(2,1)} %tokens.1, s32[1]{0:T(128)S(6)} %copy.13.counts, s32[6,512]{1,0:T(8,128)} %face_owner.1, s32[6,512]{1,0:T(8,128)} %face_row.1, s32[1,512]{1,0:T(1,128)} %bitcast.1, bf16[1,768]{1,0:T(2,128)(2,1)} %broadcast_in_dim.7.gain, bf16[768,384]{1,0:T(8,128)(2,1)} %mix_w.1, ...), custom_call_target="tpu_custom_call" | custom-call | tf_op jit(solution)/shard_map/pallas_call | solution.py:321
  77.7 1.8 %copy.14 = bf16[512,384]{1,0:T(8,128)(2,1)} copy(bf16[512,384]{1,0:T(8,128)(2,1)} %shard_map.109) | data formatting | bytes 786432
Async XLA Ops:
  0.0 0.7 copy-start

commit v3 on v2

--- a/solution.py
+++ b/solution.py
@@ -119,15 +119,17 @@
     sum_copy.start()
     mix_copy.wait()
     sum_copy.wait()
-    stream = own_rows[...].astype(F32) + jnp.dot(
-        summed[my_rows, :], mix_full[...], preferred_element_type=F32
-    )
-    own_rows[...] = stream.astype(BF16)
-    stream = own_rows[...].astype(F32)
-    var = jnp.mean(stream * stream, axis=-1, keepdims=True)
-    all_normed[b, my_rows, :] = (stream * lax.rsqrt(var + 1e-05) * gain[...].astype(F32)).astype(
-        BF16
-    )
+    def finish(ch):
+        stream = own_rows[ch * piece : (ch + 1) * piece, :].astype(F32) + jnp.dot(
+            summed[pl.ds(pl.multiple_of(c * half_r + ch * piece, piece), piece), :],
+            mix_full[...], preferred_element_type=F32,
+        )
+        own_rows[ch * piece : (ch + 1) * piece, :] = stream.astype(BF16)
+        stream = own_rows[ch * piece : (ch + 1) * piece, :].astype(F32)
+        var = jnp.mean(stream * stream, axis=-1, keepdims=True)
+        all_normed[b, pl.ds(pl.multiple_of(c * half_r + ch * piece, piece), piece), :] = (
+            stream * lax.rsqrt(var + 1e-05) * gain[...].astype(F32)
+        ).astype(BF16)
 
     def chunk(block, ch):
         return all_normed.at[block, pl.ds(pl.multiple_of(c * half_r + ch * piece, piece), piece)]
@@ -171,16 +173,17 @@
         if not first:
             z_copy(block, ch, 1).wait_recv()
 
-        @pl.when((z <= zi) & (zi < nz - 1))
-        def _():
-            z_copy(block, ch, 1).start()
-
-        @pl.when((z >= zi) & (zi > 0))
-        def _():
-            z_copy(block, ch, 0).start()
-
         if lanes_y > 1:
             y_copy(block, ch).start()
+
+        @pl.when((z <= zi) & (zi < nz - 1))
+        def _():
+            z_copy(block, ch, 1).start()
+
+        @pl.when((z >= zi) & (zi > 0))
+        def _():
+            z_copy(block, ch, 0).start()
+
         sib_copy(block, ch).start()
 
     def across(k, ch):
@@ -221,7 +224,9 @@
                 vt[h], probs, preferred_element_type=F32
             )
 
+    finish(0)
     on_line(0, 0, True)
+    finish(1)
     on_line(0, 1, True)
     stream_half[my_rows, :] = own_rows[:, my_cols]
     stream_copy = remote(

time: 79.8 us -> 79.5 us (level)
  no operation moved by 1% of the time
where the time goes in v3:
time: 79.5 us; the launch traced here: 79.2 us
  Pallas kernels  76.2 us (96%)
  local copies, waits for them, and re-layouts  2.38 us (3%)
    pallas_call x1, Pallas kernels, local(): pl.pallas_call(functools.partial(kernel, n, lanes_y), out_shape=jax.Shape...  76.2 us
    unnamed x3, local copies, waits for them, and re-layouts  1.8 us

profile of v3, /device:TPU:0, one launch (start us, length us, event | category | flops | bytes accessed | tf_op | source)
XLA Modules:
  0.0 79.2 jit_solution(17515929566024106306)
XLA Ops:
  0.0 0.0 copy-start
  0.7 0.0 copy-done
  0.7 0.6 broadcast_in_dim.7.gain
  1.3 76.2 %shard_map.109 = bf16[512,384]{1,0:T(8,128)(2,1)} custom-call(bf16[512,768]{1,0:T(8,128)(2,1)} %tokens.1, s32[1]{0:T(128)S(6)} %copy.13.counts, s32[6,512]{1,0:T(8,128)} %face_owner.1, s32[6,512]{1,0:T(8,128)} %face_row.1, s32[1,512]{1,0:T(1,128)} %bitcast.1, bf16[1,768]{1,0:T(2,128)(2,1)} %broadcast_in_dim.7.gain, bf16[768,384]{1,0:T(8,128)(2,1)} %mix_w.1, ...), custom_call_target="tpu_custom_call" | custom-call | tf_op jit(solution)/shard_map/pallas_call | solution.py:326
  77.4 1.8 %copy.14 = bf16[512,384]{1,0:T(8,128)(2,1)} copy(bf16[512,384]{1,0:T(8,128)(2,1)} %shard_map.109) | data formatting | bytes 786432
Async XLA Ops:
  0.0 0.7 copy-start
